TPU v7x, 32 devices: a whole 2x2x4 slice. The times are simulated.
32 devices in a mesh: dp: 16 (over z, y, x), shard: 2 (over core).
Axes of the slice: x: 2, y: 2, z: 4, core: 2. Of those that a mesh axis runs over, the one named last changes fastest.
Arguments:
- activations: bfloat16 [16384, 1984], P('dp'), may hold values from -6 to 6
- out_grads: bfloat16 [16384, 1984], P('dp', 'shard'), may hold values from -1.1953125 to 1.1953125
- error_state: bfloat16 [31744, 1984], P('dp', 'shard'), may hold values from -4 to 4
- basis: float32 [1984, 128], P('shard'), may hold values from -0.125 to 0.125
- master: float32 [1984, 1984], P('dp', 'shard'), may hold values from -0.125 to 0.125
- first_moment: float32 [1984, 1984], P('dp', 'shard'), may hold values from -0.3 to 0.3
- second_moment: float32 [1984, 1984], P('dp', 'shard'), may hold values from 0.0001 to 0.01
Outputs:
- new_params: bfloat16 [1984, 1984], P('dp')
- new_error: bfloat16 [31744, 1984], P('dp', 'shard')
- update: float32 [1984, 1984], P('dp', 'shard')
- new_first: float32 [1984, 1984], P('dp', 'shard')
- new_second: float32 [1984, 1984], P('dp', 'shard')
- new_master: float32 [1984, 1984], P('dp', 'shard')
- new_basis: float32 [1984, 128], P('shard')
All inputs are finite; a program needn't handle non-finite values.
Results may differ from a plain program's by a relative error of at most 0.0004.
Values may be sent and summed in bfloat16 or wider, within the bound.
A program may use at most 128 MiB of HBM per device.

v0:
```python
import jax
import jax.numpy as jnp
from jax import lax
from jax.sharding import PartitionSpec as P

beta_one = 0.9
beta_two = 0.95
step_size = 0.001
adam_epsilon = 1e-08
ridge_scale = 1e-06
highest = lax.Precision.HIGHEST


def solve_rows(gram_matrix, row_piece):
    width = gram_matrix.shape[0]
    ridge_term = (
        ridge_scale * jnp.trace(gram_matrix) / width * jnp.eye(width, dtype=gram_matrix.dtype)
    )
    factor = jnp.linalg.cholesky(gram_matrix + ridge_term)
    return jax.scipy.linalg.solve_triangular(factor, row_piece.T, lower=True).T


def per_device(activations, out_grads, error_state, basis, master, first_moment, second_moment):
    product = lax.dot_general(
        activations, out_grads, (((0,), (0,)), ((), ())), preferred_element_type=jnp.float32
    )
    merged = product + error_state.astype(jnp.float32)
    rows_dev = master.shape[0]
    partial_value = jnp.dot(merged, basis, precision=highest)
    summed = lax.psum(partial_value, ("dp", "shard"))
    gram_matrix = jnp.dot(summed.T, summed, precision=highest)
    orthonormal = solve_rows(gram_matrix, summed)
    local_right = lax.dot_general(merged, orthonormal, (((0,), (0,)), ((), ())), precision=highest)
    new_basis = lax.psum(local_right, "dp") / lax.axis_size("dp")
    decompressed = lax.dot_general(
        orthonormal, new_basis, (((1,), (1,)), ((), ())), precision=highest
    )
    new_error = (merged - decompressed).astype(jnp.bfloat16)
    row_offset = lax.axis_index("dp") * rows_dev
    update = lax.dynamic_slice_in_dim(decompressed, row_offset, rows_dev, 0)
    new_first = beta_one * first_moment + (1.0 - beta_one) * update
    new_second = beta_two * second_moment + (1.0 - beta_two) * update * update
    new_master = master - step_size * new_first / (jnp.sqrt(new_second) + adam_epsilon)
    new_params = lax.all_gather(new_master.astype(jnp.bfloat16), "shard", axis=1, tiled=True)
    return (new_params, new_error, update, new_first, new_second, new_master, new_basis)


def solution(mesh):
    placed = (
        P("dp", None),
        P("dp", "shard"),
        P("dp", "shard"),
        P("shard", None),
        P("dp", "shard"),
        P("dp", "shard"),
        P("dp", "shard"),
    )
    return jax.shard_map(
        per_device,
        mesh=mesh,
        in_specs=placed,
        out_specs=(
            P("dp", None),
            P("dp", "shard"),
            P("dp", "shard"),
            P("dp", "shard"),
            P("dp", "shard"),
            P("dp", "shard"),
            P("shard", None),
        ),
        check_vma=False,
    )
```

profile of v0, /device:TPU:0, one launch (start us, length us, event | category | flops | bytes accessed | tf_op | source)
XLA Modules:
  0.0 356.9 jit_solution(4168501354691575905)
XLA Ops:
  7.2 0.0 all-reduce.3.cloned.1.call-start
  7.2 1.5 copy-done
  8.7 10.1 %convert_add_fusion = f32[1984,992]{1,0:T(8,128)S(1)} fusion(bf16[1984,992]{1,0:T(8,128)(2,1)} %param.9, bf16[1024,1984]{0,1:T(8,128)(2,1)} %param.7, bf16[1024,992]{0,1:T(8,128)(2,1)S(1)} %copy-done), kind=kOutput, calls=%fused_computation.1 | convolution fusion | flops 4034662400 | bytes 17903616 | tf_op jit(solution)/shard_map/dot_general | solution.py:24
  18.9 3.1 copy-done.1
  22.0 7.6 %fusion.8 = f32[1984,128]{1,0:T(8,128)} fusion(f32[1984,992]{1,0:T(8,128)S(1)} %convert_add_fusion, f32[992,128]{1,0:T(8,128)S(1)} %copy-done.3), kind=kOutput, calls=%fused_computation.22 | convolution fusion | flops 3023044608 | bytes 9396224 | tf_op jit(solution)/shard_map/dot_general | solution.py:29
  29.7 0.0 all-reduce.3.cloned.1.call-update
  29.7 0.2 all-reduce.5.cloned.1.call-start
  29.9 131.7 %all-reduce.3.cloned.1.call-done = f32[1984,128]{1,0:T(8,128)} async-done(((f32[1984,128]{1,0:T(8,128)}), f32[1984,128]{1,0:T(8,128)}) %all-reduce.3.cloned.1.call-update) | async-done | bytes 1015824 | tf_op jit(solution)/shard_map/psum | solution.py:30
  161.6 4.0 %select_reduce_fusion.1 = (f32[]{:T(128)}, f32[128,128]{1,0:T(8,128)S(1)}) fusion(f32[1984,128]{1,0:T(8,128)} %all-reduce.3.cloned.1.call-done), kind=kOutput, calls=%fused_computation.16 | convolution fusion | flops 390119424 | bytes 1081348 | tf_op jit(solution)/shard_map/dot_general | solution.py:31
  165.7 0.1 copy.14
  166.5 11.7 %cholesky.17 = f32[128,128]{1,0:T(8,128)S(1)} custom-call(f32[128,128]{1,0:T(8,128)S(1)} %fusion.5), custom_call_target="Cholesky" | custom-call | tf_op jit(solution)/shard_map/jit(cholesky)/cholesky | solution.py:19
  178.2 0.6 compare_reduce_fusion
  178.8 0.7 fusion.1
  179.5 9.8 %custom-call.7 = f32[1,128,128]{1,2,0:T(8,128)S(1)} custom-call(f32[1,128,128]{2,1,0:T(8,128)S(1)} %fusion.1), custom_call_target="InvertDiagBlocksLowerTriangular" | custom-call | tf_op jit(solution)/shard_map/jit(_solve_triangular)/triangular_solve | solution.py:20
  189.3 2.2 fusion.2
  191.5 16.5 %fusion.9 = f32[992,128]{1,0:T(8,128)} fusion(f32[1984,992]{1,0:T(8,128)} %copy-done.1, f32[128,1984]{0,1:T(8,128)S(1)} %fusion.2), kind=kOutput, calls=%fused_computation.23 | convolution fusion | flops 3023044608 | bytes 9396224 | tf_op jit(solution)/shard_map/dot_general | solution.py:33
  208.0 107.9 %all-reduce.5.cloned.1.call-done = f32[992,128]{1,0:T(8,128)} async-done(((f32[992,128]{1,0:T(8,128)}), f32[992,128]{1,0:T(8,128)}) %all-reduce.5.cloned.1.call-update) | async-done | bytes 507920 | tf_op jit(solution)/shard_map/psum | solution.py:34
  315.9 1.1 broadcast_multiply_fusion
  317.0 8.8 %fusion.10 = f32[1984,992]{0,1:T(8,128)} fusion(f32[128,1984]{0,1:T(8,128)S(1)} %fusion.2, f32[992,128]{1,0:T(8,128)S(1)} %broadcast_multiply_fusion), kind=kOutput, calls=%fused_computation.24 | convolution fusion | flops 3023044608 | bytes 9396224 | tf_op jit(solution)/shard_map/dot_general | solution.py:35
  325.8 9.1 %copy.15 = f32[1984,992]{1,0:T(8,128)} copy(f32[1984,992]{0,1:T(8,128)} %fusion.10) | data formatting | bytes 15745024 | tf_op jit(solution)/shard_map/dot_general | solution.py:35
  334.9 9.3 %subtract_convert_fusion = bf16[1984,992]{1,0:T(8,128)(2,1)} fusion(f32[1984,992]{1,0:T(8,128)} %copy-done.1, f32[1984,992]{1,0:T(8,128)} %copy.15), kind=kLoop, calls=%fused_computation | loop fusion | flops 3936256 | bytes 19681280 | tf_op jit(solution)/shard_map/convert_element_type | solution.py:38
  344.3 2.9 fusion.6
  347.1 2.2 all_gather.3
  349.3 0.8 copy.19
  (15 shorter events, 0.1 us)
Async XLA Ops:
  7.2 1.6 copy-start
  7.2 14.8 %copy-start.3 = (f32[992,128]{1,0:T(8,128)S(1)}, f32[992,128]{1,0:T(8,128)}, u32[]{:S(2)}) copy-start(f32[992,128]{1,0:T(8,128)} %param.10) | copy-start | bytes 1523716
  7.2 154.4 %all-reduce.3.cloned.1.call-start = ((), (), s32[]{:S(2)}) async-start(), calls=%async_computation | async-start | bytes 2031616 | tf_op jit(solution)/shard_map/psum | solution.py:30
  18.9 3.1 copy-start.1
  29.7 286.3 %all-reduce.5.cloned.1.call-start = ((), (), s32[]{:S(2)}) async-start(), calls=%async_computation.1 | async-start | bytes 1015808 | tf_op jit(solution)/shard_map/psum | solution.py:34
  317.0 17.9 %copy-start.2 = (f32[992,128]{1,0:T(8,128)}, f32[992,128]{1,0:T(8,128)S(1)}, u32[]{:S(2)}) copy-start(f32[992,128]{1,0:T(8,128)S(1)} %broadcast_multiply_fusion) | copy-start | bytes 1523716
  334.9 9.3 %copy-start.4 = (f32[124,992]{0,1:T(8,128)S(1)}, f32[124,992]{0,1:T(8,128)}, u32[]{:S(2)}) copy-start(f32[124,992]{0,1:T(8,128)} %param.11) | copy-start | bytes 1476100
  334.9 9.3 %copy-start.5 = (f32[124,992]{0,1:T(8,128)S(1)}, f32[124,992]{0,1:T(8,128)}, u32[]{:S(2)}) copy-start(f32[124,992]{0,1:T(8,128)} %param.12) | copy-start | bytes 1476100
  334.9 9.3 %copy-start.6 = (f32[124,992]{0,1:T(8,128)S(1)}, f32[124,992]{0,1:T(8,128)}, u32[]{:S(2)}) copy-start(f32[124,992]{0,1:T(8,128)} %param.13) | copy-start | bytes 1476100
Sparse Core Ops, SparseCore 0:
  29.8 131.7 all-reduce.2
  208.1 107.7 all-reduce.4
where the time goes:
time: 357 us
  waiting for transfers between devices  240 us (67%)
  matrix products  49.2 us (14%)
  other arithmetic  36.1 us (10%)
  between operations  14.8 us (4%)
  local copies, waits for them, and re-layouts  14.6 us (4%)
    psum x1, waiting for transfers between devices, per_device(): summed = lax.psum(partial_value, ('dp', 'shard'))  132 us
    psum x1, waiting for transfers between devices, per_device(): new_basis = lax.psum(local_right, 'dp') / lax.axis_size('dp')  108 us
    dot_general x1, matrix products, per_device(): lax.dot_general(merged, orthonormal, (((0,), (0,)), ((), ())), precision=...  16.5 us
    another operation x3, other arithmetic, solve_rows(): factor = jnp.linalg.cholesky(gram_matrix + ridge_term)  12.4 us
    another operation x2, other arithmetic, solve_rows(): return jax.scipy.linalg.solve_triangular(factor, row_piece.T, lower=True).T  10.5 us
    dot_general x1, matrix products, per_device(): lax.dot_general(activations, out_grads, (((0,), (0,)), ((), ())), preferr...  10.1 us
    convert_element_type x1, other arithmetic, per_device(): new_error = (merged - decompressed).astype(jnp.bfloat16)  9.33 us
    dot_general x1, local copies, waits for them, and re-layouts, per_device(): lax.dot_general(orthonormal, new_basis, (((1,), (1,)), ((), ())), precisi...  9.12 us
  transfers between devices with their start and end apart: 2, of which 2 were waited for; matrix products, arithmetic and copies ran while one was open for 0% of the time, Pallas kernels for 0%

commit v1 on v0

v1 whole, which is shorter than its diff:
```python
import functools

import jax
import jax.numpy as jnp
from jax import lax
from jax.experimental import pallas as pl
from jax.experimental.pallas import tpu as pltpu
from jax.sharding import PartitionSpec as P

beta_one = 0.9
beta_two = 0.95
step_size = 0.001
adam_epsilon = 1e-08
ridge_scale = 1e-06
highest = lax.Precision.HIGHEST
high = lax.Precision.HIGH
MESH = pl.DeviceIdType.MESH


def solve_rows(gram_matrix, row_piece):
    width = gram_matrix.shape[0]
    ridge_term = (
        ridge_scale * jnp.trace(gram_matrix) / width * jnp.eye(width, dtype=gram_matrix.dtype)
    )
    factor = jnp.linalg.cholesky(gram_matrix + ridge_term)
    return jax.scipy.linalg.solve_triangular(factor, row_piece.T, lower=True).T


def adam(update, master, first_moment, second_moment):
    new_first = beta_one * first_moment + (1.0 - beta_one) * update
    new_second = beta_two * second_moment + (1.0 - beta_two) * update * update
    new_master = master - step_size * new_first / (jnp.sqrt(new_second) + adam_epsilon)
    return new_first, new_second, new_master


def rows_at(index, size):
    return pl.ds(pl.multiple_of(index * size, size), size)


def greet(minor, major, pair):
    dp, core = lax.axis_index("dp"), lax.axis_index("shard")
    q, z = lax.rem(dp, minor), lax.div(dp, minor)
    barrier = pltpu.get_barrier_semaphore()
    count = 0
    if pair:
        pl.semaphore_signal(
            barrier, inc=1, device_id={"dp": dp, "shard": 1 - core}, device_id_type=MESH
        )
        count += 1
    for j in range(1, minor):
        peer = z * minor + lax.rem(q + j, minor)
        pl.semaphore_signal(
            barrier, inc=1, device_id={"dp": peer, "shard": core}, device_id_type=MESH
        )
        count += 1
    for j in range(1, major):
        peer = lax.rem(z + j, major) * minor + q
        pl.semaphore_signal(
            barrier, inc=1, device_id={"dp": peer, "shard": core}, device_id_type=MESH
        )
        count += 1
    pl.semaphore_wait(barrier, count)


def push(src, dst, send, recv, slot, dp, core):
    copy = pltpu.make_async_remote_copy(
        src_ref=src,
        dst_ref=dst,
        send_sem=send.at[slot],
        recv_sem=recv.at[slot],
        device_id={"dp": dp, "shard": core},
        device_id_type=MESH,
    )
    copy.start()
    return copy


def scatter_minor(minor, source, land, send, recv, slot):
    dp, core = lax.axis_index("dp"), lax.axis_index("shard")
    q, z = lax.rem(dp, minor), lax.div(dp, minor)
    size = source.shape[0] // minor
    copies = []
    for j in range(1, minor):
        to = lax.rem(q + j, minor)
        copies.append(
            push(source.at[rows_at(to, size)], land.at[j - 1], send, recv, slot + j - 1,
                 z * minor + to, core)
        )
    return copies


def scatter_major(minor, major, source, land, send, recv, slot):
    dp, core = lax.axis_index("dp"), lax.axis_index("shard")
    q, z = lax.rem(dp, minor), lax.div(dp, minor)
    size = source.shape[0] // major
    copies = []
    for j in range(1, major):
        to = lax.rem(z + j, major)
        copies.append(
            push(source.at[rows_at(to, size)], land.at[j - 1], send, recv, slot + j - 1,
                 to * minor + q, core)
        )
    return copies


def gather(minor, major, along_major, ref, rows, send, recv, slot):
    dp, core = lax.axis_index("dp"), lax.axis_index("shard")
    q, z = lax.rem(dp, minor), lax.div(dp, minor)
    copies = []
    for j in range(1, major if along_major else minor):
        if along_major:
            peer = lax.rem(z + j, major) * minor + q
        else:
            peer = z * minor + lax.rem(q + j, minor)
        copies.append(push(ref.at[rows], ref.at[rows], send, recv, slot + j - 1, peer, core))
    return copies


def arrive(copies):
    for copy in copies:
        copy.wait()


def left_kernel(minor, major, part, total, half, quarter, land_core, land_minor, land_major,
                send, recv):
    dp, core = lax.axis_index("dp"), lax.axis_index("shard")
    q, z = lax.rem(dp, minor), lax.div(dp, minor)
    greet(minor, major, True)
    n_half = half.shape[0]
    n_quarter = quarter.shape[0]
    n_own = n_quarter // major
    arrive([push(part.at[rows_at(1 - core, n_half)], land_core, send, recv, 0, dp, 1 - core)])
    half[...] = part[rows_at(core, n_half), :] + land_core[...]
    arrive(scatter_minor(minor, half, land_minor, send, recv, 1))
    value = half[rows_at(q, n_quarter), :]
    for j in range(minor - 1):
        value = value + land_minor[j]
    quarter[...] = value
    slot = minor
    arrive(scatter_major(minor, major, quarter, land_major, send, recv, slot))
    slot += major - 1
    value = quarter[rows_at(z, n_own), :]
    for j in range(major - 1):
        value = value + land_major[j]
    own = rows_at((core * minor + q) * major + z, n_own)
    total[own, :] = value
    arrive(gather(minor, major, True, total, own, send, recv, slot))
    slot += major - 1
    own = rows_at(core * minor + q, n_quarter)
    arrive(gather(minor, major, False, total, own, send, recv, slot))
    slot += minor - 1
    own = rows_at(core, n_half)
    arrive([push(total.at[own], total.at[own], send, recv, slot, dp, 1 - core)])


def sum_left(part, minor, major):
    rows, rank = part.shape
    n_half = rows // 2
    n_quarter = n_half // minor
    n_own = n_quarter // major
    copies = 2 + 2 * (minor - 1) + 2 * (major - 1)
    vmem = pl.BlockSpec(memory_space=pltpu.VMEM)
    f32 = jnp.float32
    return pl.pallas_call(
        functools.partial(left_kernel, minor, major),
        out_shape=jax.ShapeDtypeStruct((rows, rank), f32),
        in_specs=[vmem],
        out_specs=vmem,
        scratch_shapes=[
            pltpu.VMEM((n_half, rank), f32),
            pltpu.VMEM((n_quarter, rank), f32),
            pltpu.VMEM((n_half, rank), f32),
            pltpu.VMEM((minor - 1, n_quarter, rank), f32),
            pltpu.VMEM((major - 1, n_own, rank), f32),
            pltpu.SemaphoreType.DMA((copies,)),
            pltpu.SemaphoreType.DMA((copies,)),
        ],
        compiler_params=pltpu.CompilerParams(
            collective_id=0, has_side_effects=True, vmem_limit_bytes=32 * 1024 * 1024
        ),
    )(part)


def invert_factor(gram, work):
    rank = gram.shape[0]
    lane = lax.broadcasted_iota(jnp.int32, (rank, rank), 1)
    line = lax.broadcasted_iota(jnp.int32, (rank, rank), 0)
    eye = lane == line
    trace = jnp.sum(jnp.where(eye, gram, 0.0), keepdims=True)
    work[:, :rank] = gram + jnp.where(eye, ridge_scale * trace / rank, 0.0)
    work[:, rank:] = jnp.where(eye, 1.0, 0.0)

    def step(j, carry):
        row = work[pl.ds(j, 1), :]
        left = work[:, :rank]
        column = jnp.sum(jnp.where(lane == j, left, 0.0), axis=1, keepdims=True)
        pivot = jnp.sum(
            jnp.where(lane[:1] == j, row[:, :rank], 0.0), axis=1, keepdims=True
        )
        scale = jnp.where(line[:, :1] > j, column / pivot, 0.0)
        work[...] = work[...] - scale * row
        return carry

    lax.fori_loop(0, rank, step, 0)
    pivots = jnp.sum(jnp.where(eye, work[:, :rank], 0.0), axis=1, keepdims=True)
    return work[:, rank:] * lax.rsqrt(pivots)


def right_kernel(minor, major, rows, part, left, basis, ortho, quarter, land_minor, land_major,
                 total, work, inverse, send, recv):
    dp = lax.axis_index("dp")
    q, z = lax.rem(dp, minor), lax.div(dp, minor)
    greet(minor, major, False)
    n_quarter = quarter.shape[0]
    n_own = n_quarter // major
    copies = scatter_minor(minor, part, land_minor, send, recv, 0)
    summed = left[...]
    gram = lax.dot_general(
        summed, summed, (((0,), (0,)), ((), ())), precision=highest,
        preferred_element_type=jnp.float32,
    )
    inverse[...] = invert_factor(gram, work)
    ortho[...] = lax.dot_general(
        left[:rows, :], inverse[...], (((1,), (1,)), ((), ())), precision=highest,
        preferred_element_type=jnp.float32,
    )
    arrive(copies)
    value = part[rows_at(q, n_quarter), :]
    for j in range(minor - 1):
        value = value + land_minor[j]
    quarter[...] = value
    slot = minor - 1
    arrive(scatter_major(minor, major, quarter, land_major, send, recv, slot))
    slot += major - 1
    value = quarter[rows_at(z, n_own), :]
    for j in range(major - 1):
        value = value + land_major[j]
    own = rows_at(q * major + z, n_own)
    total[own, :] = value
    arrive(gather(minor, major, True, total, own, send, recv, slot))
    slot += major - 1
    own = rows_at(q, n_quarter)
    arrive(gather(minor, major, False, total, own, send, recv, slot))
    basis[...] = lax.dot_general(
        inverse[...], total[...], (((1,), (0,)), ((), ())), precision=highest,
        preferred_element_type=jnp.float32,
    ) * (1.0 / (minor * major))


def sum_right(part, left, rows, minor, major):
    rank, columns = part.shape
    n_quarter = rank // minor
    n_own = n_quarter // major
    copies = 2 * (minor - 1) + 2 * (major - 1)
    vmem = pl.BlockSpec(memory_space=pltpu.VMEM)
    f32 = jnp.float32
    return pl.pallas_call(
        functools.partial(right_kernel, minor, major, rows),
        out_shape=(
            jax.ShapeDtypeStruct((rank, columns), f32),
            jax.ShapeDtypeStruct((rows, rank), f32),
        ),
        in_specs=[vmem, vmem],
        out_specs=(vmem, vmem),
        scratch_shapes=[
            pltpu.VMEM((n_quarter, columns), f32),
            pltpu.VMEM((minor - 1, n_quarter, columns), f32),
            pltpu.VMEM((major - 1, n_own, columns), f32),
            pltpu.VMEM((rank, columns), f32),
            pltpu.VMEM((rank, 2 * rank), f32),
            pltpu.VMEM((rank, rank), f32),
            pltpu.SemaphoreType.DMA((copies,)),
            pltpu.SemaphoreType.DMA((copies,)),
        ],
        compiler_params=pltpu.CompilerParams(
            collective_id=1, has_side_effects=True, vmem_limit_bytes=48 * 1024 * 1024
        ),
    )(part, left)


def pushed(minor, major, activations, out_grads, error_state, basis, master, first_moment,
           second_moment):
    product = lax.dot_general(
        activations, out_grads, (((0,), (0,)), ((), ())), preferred_element_type=jnp.float32
    )
    merged = product + error_state.astype(jnp.float32)
    rows = merged.shape[0]
    chunk = 16 * minor * major
    padded = -(-rows // chunk) * chunk
    part = jnp.dot(merged, basis, precision=high)
    left = sum_left(jnp.pad(part, ((0, padded - rows), (0, 0))), minor, major)
    right = lax.dot_general(left[:rows], merged, (((0,), (0,)), ((), ())), precision=high)
    basis_rows, orthonormal = sum_right(right, left, rows, minor, major)
    decompressed = jnp.dot(orthonormal, basis_rows, precision=high)
    new_error = (merged - decompressed).astype(jnp.bfloat16)
    rows_dev = master.shape[0]
    row_offset = lax.axis_index("dp") * rows_dev
    update = jnp.dot(
        lax.dynamic_slice_in_dim(orthonormal, row_offset, rows_dev, 0), basis_rows, precision=high
    )
    new_first, new_second, new_master = adam(update, master, first_moment, second_moment)
    new_params = lax.all_gather(new_master.astype(jnp.bfloat16), "shard", axis=1, tiled=True)
    return (new_params, new_error, update, new_first, new_second, new_master, basis_rows.T)


def summed_by_psum(activations, out_grads, error_state, basis, master, first_moment,
                   second_moment):
    product = lax.dot_general(
        activations, out_grads, (((0,), (0,)), ((), ())), preferred_element_type=jnp.float32
    )
    merged = product + error_state.astype(jnp.float32)
    rows_dev = master.shape[0]
    partial_value = jnp.dot(merged, basis, precision=highest)
    summed = lax.psum(partial_value, ("dp", "shard"))
    gram_matrix = jnp.dot(summed.T, summed, precision=highest)
    orthonormal = solve_rows(gram_matrix, summed)
    local_right = lax.dot_general(merged, orthonormal, (((0,), (0,)), ((), ())), precision=highest)
    new_basis = lax.psum(local_right, "dp") / lax.axis_size("dp")
    decompressed = lax.dot_general(
        orthonormal, new_basis, (((1,), (1,)), ((), ())), precision=highest
    )
    new_error = (merged - decompressed).astype(jnp.bfloat16)
    row_offset = lax.axis_index("dp") * rows_dev
    update = lax.dynamic_slice_in_dim(decompressed, row_offset, rows_dev, 0)
    new_first, new_second, new_master = adam(update, master, first_moment, second_moment)
    new_params = lax.all_gather(new_master.astype(jnp.bfloat16), "shard", axis=1, tiled=True)
    return (new_params, new_error, update, new_first, new_second, new_master, new_basis)


def solution(mesh):
    replicas, shards = mesh.shape["dp"], mesh.shape["shard"]
    minor = 1
    while minor * minor < replicas:
        minor *= 2
    major = replicas // minor
    placed = (
        P("dp", None),
        P("dp", "shard"),
        P("dp", "shard"),
        P("shard", None),
        P("dp", "shard"),
        P("dp", "shard"),
        P("dp", "shard"),
    )

    def step(activations, out_grads, error_state, basis, master, first_moment, second_moment):
        if shards == 2 and minor * major == replicas and basis.shape[1] % (8 * replicas) == 0:
            body = functools.partial(pushed, minor, major)
        else:
            body = summed_by_psum
        return jax.shard_map(
            body,
            mesh=mesh,
            in_specs=placed,
            out_specs=(
                P("dp", None),
                P("dp", "shard"),
                P("dp", "shard"),
                P("dp", "shard"),
                P("dp", "shard"),
                P("dp", "shard"),
                P("shard", None),
            ),
            check_vma=False,
        )(activations, out_grads, error_state, basis, master, first_moment, second_moment)

    return step
```

time: 357 us -> 97.1 us (0.27)
  waiting for transfers between devices: 240 us -> 0 us
  Pallas kernels: 0 us -> 65.9 us
  other arithmetic: 36.1 us -> 0 us
  matrix products: 49.2 us -> 23.8 us
  between operations: 14.8 us -> 0.72 us
  local copies, waits for them, and re-layouts: 14.6 us -> 4.36 us
    psum x2 -> x0, waiting for transfers between devices: 240 us -> none  [the longest x1 132 us: per_device(): summed = lax.psum(partial_value, ('dp', 'shard'))]
    pallas_call x0 -> x2, Pallas kernels: none -> 65.9 us  [the longest x1 34.5 us: sum_right(): pl.pallas_call(functools.partial(right_kernel, minor, major, rows), out_s...]
    dot_general x5, matrix products: 47.1 us -> 23.8 us  [the longest x1 10 us: pushed(): lax.dot_general(activations, out_grads, (((0,), (0,)), ((), ())), preferr...]
    another operation x5 -> x0, other arithmetic: 22.9 us -> none  [the longest x3 12.4 us: solve_rows(): factor = jnp.linalg.cholesky(gram_matrix + ridge_term)]
    convert_element_type x2 -> x0, other arithmetic: 12.2 us -> none  [the longest x1 9.33 us: per_device(): new_error = (merged - decompressed).astype(jnp.bfloat16)]
    dot_general x2 -> x0, local copies, waits for them, and re-layouts: 9.21 us -> none  [the longest x1 9.12 us: per_device(): lax.dot_general(orthonormal, new_basis, (((1,), (1,)), ((), ())), precisi...]
  transfers between devices with their start and end apart: 2 -> 0, of which waited for: 2 -> 0; matrix products, arithmetic and copies ran while one was open for 0% -> 0% of each run, Pallas kernels for 0% -> 0%
where the time goes in v1:
time: 97.1 us; the launch traced here: 97 us
  Pallas kernels  65.9 us (68%)
  matrix products  23.8 us (25%)
  local copies, waits for them, and re-layouts  4.36 us (4%)
  blocking collectives  2.16 us (2%)
    pallas_call x1, Pallas kernels, sum_right(): pl.pallas_call(functools.partial(right_kernel, minor, major, rows), out_s...  34.5 us
    pallas_call x1, Pallas kernels, sum_left(): pl.pallas_call(functools.partial(left_kernel, minor, major), out_shape=ja...  31.4 us
    dot_general x1, matrix products, pushed(): lax.dot_general(activations, out_grads, (((0,), (0,)), ((), ())), preferr...  10 us
    dot_general x1, matrix products, pushed(): decompressed = jnp.dot(orthonormal, basis_rows, precision=high)  4.89 us
    unnamed x10, local copies, waits for them, and re-layouts  4.29 us
    dot_general x1, matrix products, pushed(): part = jnp.dot(merged, basis, precision=high)  3.33 us
    dot_general x1, matrix products, pushed(): jnp.dot(lax.dynamic_slice_in_dim(orthonormal, row_offset, rows_dev, 0), b...  3.24 us
    dot_general x1, matrix products, pushed(): lax.dot_general(left[:rows], merged, (((0,), (0,)), ((), ())), precision=...  2.36 us

profile of v1, /device:TPU:0, one launch (start us, length us, event | category | flops | bytes accessed | tf_op | source)
XLA Modules:
  0.0 97.0 jit_solution(5880605663469739303)
XLA Ops:
  0.6 0.0 copy-start
  0.7 1.6 %copy-done = bf16[1024,992]{0,1:T(8,128)(2,1)S(1)} copy-done((bf16[1024,992]{0,1:T(8,128)(2,1)S(1)}, bf16[1024,992]{0,1:T(8,128)(2,1)}, u32[]{:S(2)}) %copy-start) | copy-done | bytes 2031640
  2.2 0.0 copy-start.2
  2.2 10.0 %convert_add_fusion = f32[1984,992]{1,0:T(8,128)S(1)} fusion(bf16[1984,992]{1,0:T(8,128)(2,1)} %param.9, bf16[1024,1984]{0,1:T(8,128)(2,1)} %param.7, bf16[1024,992]{0,1:T(8,128)(2,1)S(1)} %copy-done), kind=kOutput, calls=%fused_computation.1 | convolution fusion | flops 4034662400 | bytes 17903616 | tf_op jit(solution)/shard_map/dot_general | solution.py:283
  12.2 0.0 copy-done.2
  12.2 3.3 %fusion.8 = f32[1984,128]{1,0:T(8,128)S(1)} fusion(f32[1984,992]{1,0:T(8,128)S(1)} %convert_add_fusion, f32[992,128]{1,0:T(8,128)S(1)} %copy-done.2), kind=kOutput, calls=%fused_computation.12 | convolution fusion | flops 1511522304 | bytes 9396224 | tf_op jit(solution)/shard_map/dot_general | solution.py:290
  15.6 0.1 pad.4.part
  15.7 31.4 %shard_map.126.left = f32[2048,128]{1,0:T(8,128)S(1)} custom-call(f32[2048,128]{1,0:T(8,128)S(1)} %pad.4.part), custom_call_target="tpu_custom_call" | custom-call | tf_op jit(solution)/shard_map/pallas_call | solution.py:164
  47.1 2.4 %fusion.part = f32[128,992]{1,0:T(8,128)S(1)} fusion(f32[1984,992]{1,0:T(8,128)S(1)} %convert_add_fusion, f32[2048,128]{1,0:T(8,128)S(1)} %shard_map.126.left), kind=kOutput, calls=%fused_computation.2 | convolution fusion | flops 1511522304 | bytes 9650176 | tf_op jit(solution)/shard_map/dot_general | solution.py:292
  49.4 0.0 copy-start.3
  49.5 34.5 %shard_map.127 = (f32[128,992]{1,0:T(8,128)S(1)}, f32[1984,128]{1,0:T(8,128)S(1)}) custom-call(f32[128,992]{1,0:T(8,128)S(1)} %fusion.part, f32[2048,128]{1,0:T(8,128)S(1)} %shard_map.126.left), custom_call_target="tpu_custom_call" | custom-call | tf_op jit(solution)/shard_map/pallas_call | solution.py:257
  83.9 0.0 copy-start.1
  84.0 0.9 copy-done.1
  84.9 4.9 %subtract_convert_fusion = bf16[1984,992]{1,0:T(8,128)(2,1)} fusion(f32[1984,992]{1,0:T(8,128)S(1)} %convert_add_fusion, f32[1984,128]{1,0:T(8,128)S(1)} %get-tuple-element.9, f32[128,992]{1,0:T(8,128)S(1)} %get-tuple-element.10), kind=kOutput, calls=%fused_computation | convolution fusion | flops 1515458560 | bytes 13332480 | tf_op jit(solution)/shard_map/dot_general | solution.py:294
  89.8 1.0 %copy.15 = f32[992,128]{1,0:T(8,128)} copy(f32[992,128]{0,1:T(8,128)S(1)} %bitcast.9) | data formatting | bytes 1015808
  90.8 0.0 copy-done.3
  90.8 3.2 %fusion.6 = (bf16[124,992]{0,1:T(8,128)(2,1)S(1)}, f32[124,992]{0,1:T(8,128)}, f32[124,992]{0,1:T(8,128)}, f32[124,992]{0,1:T(8,128)}, f32[124,992]{0,1:T(8,128)}) fusion(f32[124,992]{0,1:T(8,128)S(1)} %copy-done.3, f32[124,992]{0,1:T(8,128)} %param.12, f32[124,992]{0,1:T(8,128)} %param.13, f32[128,992]{1,0:T(8,128)S(1)} %get-tuple-element.10, ...), kind=kOutput, calls=%fused_computation.11 | convolution fusion | flops 95946240 | bytes 4295428 | tf_op jit(solution)/shard_map/dot_general | solution.py:298
  94.0 2.2 %all_gather.3 = bf16[124,1984]{0,1:T(8,128)(2,1)S(1)} all-gather(bf16[124,992]{0,1:T(8,128)(2,1)S(1)} %get-tuple-element.18), channel_id=1, replica_groups=mesh['dp'=16,'shard'=2] {'shard'}, dimensions={1}, use_global_device_ids=true | all-gather | bytes 738048 | tf_op jit(solution)/shard_map/all_gather | solution.py:302
  96.2 0.8 copy.18
Async XLA Ops:
  0.6 1.6 %copy-start = (bf16[1024,992]{0,1:T(8,128)(2,1)S(1)}, bf16[1024,992]{0,1:T(8,128)(2,1)}, u32[]{:S(2)}) copy-start(bf16[1024,992]{0,1:T(8,128)(2,1)} %param.8) | copy-start | bytes 6094852
  2.2 10.0 %copy-start.2 = (f32[992,128]{1,0:T(8,128)S(1)}, f32[992,128]{1,0:T(8,128)}, u32[]{:S(2)}) copy-start(f32[992,128]{1,0:T(8,128)} %param.10) | copy-start | bytes 1523716
  49.4 41.3 %copy-start.3 = (f32[124,992]{0,1:T(8,128)S(1)}, f32[124,992]{0,1:T(8,128)}, u32[]{:S(2)}) copy-start(f32[124,992]{0,1:T(8,128)} %param.11) | copy-start | bytes 1476100
  83.9 1.0 copy-start.1

commit v2 on v1

--- a/solution.py
+++ b/solution.py
@@ -121,176 +121,272 @@
         copy.wait()
 
 
-def left_kernel(minor, major, part, total, half, quarter, land_core, land_minor, land_major,
-                send, recv):
+def halves(value):
+    top = value.astype(jnp.bfloat16)
+    rest = (value - top.astype(jnp.float32)).astype(jnp.bfloat16)
+    return jnp.concatenate([top, rest], axis=0)
+
+
+def fold(value):
+    rank = value.shape[0] // 2
+    return value[:rank] + value[rank:]
+
+
+def dot(left, right, left_dim, right_dim, precision=None):
+    return lax.dot_general(
+        left, right, (((left_dim,), (right_dim,)), ((), ())), precision=precision,
+        preferred_element_type=jnp.float32,
+    )
+
+
+def begin_factor(gram, work):
+    rank = gram.shape[0]
+    lane = lax.broadcasted_iota(jnp.int32, (rank, rank), 1)
+    line = lax.broadcasted_iota(jnp.int32, (rank, rank), 0)
+    trace = jnp.sum(jnp.where(lane == line, gram, 0.0), keepdims=True)
+    work[...] = gram + jnp.where(lane == line, ridge_scale * trace / rank, 0.0)
+
+
+def eliminate(work, first, last):
+    rank = work.shape[0]
+    lane = lax.broadcasted_iota(jnp.int32, (rank, rank), 1)
+    line = lax.broadcasted_iota(jnp.int32, (rank, rank), 0)
+    lane_row, line_column = lane[:1], line[:, :1]
+
+    def pick(value, index, places):
+        return jnp.sum(jnp.where(places == index, value, 0.0), axis=1, keepdims=True)
+
+    def step(pair, carry):
+        j = 2 * pair
+        k = j + 1
+        matrix = work[...]
+        row_j, row_k = work[pl.ds(j, 1), :], work[pl.ds(k, 1), :]
+        column_j, column_k = pick(matrix, j, lane), pick(matrix, k, lane)
+        jj, jk = pick(row_j, j, lane_row), pick(row_j, k, lane_row)
+        kj, kk = pick(row_k, j, lane_row), pick(row_k, k, lane_row)
+        inverse_j = 1.0 / jj
+        ratio = kj * inverse_j
+        inverse_k = 1.0 / (kk - ratio * jk)
+        scale_j = jnp.where(line_column > j, column_j * inverse_j, 0.0)
+        scale_k = jnp.where(line_column > k, (column_k - scale_j * jk) * inverse_k, 0.0)
+        unit_j = jnp.where(lane_row == j, 1.0, row_j)
+        unit_k = jnp.where(
+            lane_row == k, 1.0, jnp.where(lane_row == j, 0.0, row_k) - ratio * unit_j
+        )
+        matrix = jnp.where((lane == j) & (line > j), 0.0, matrix) - scale_j * unit_j
+        matrix = jnp.where((lane == k) & (line > k), 0.0, matrix) - scale_k * unit_k
+        work[...] = matrix
+        return carry
+
+    lax.fori_loop(first, last, step, 0)
+
+
+def finish_factor(work):
+    rank = work.shape[0]
+    lane = lax.broadcasted_iota(jnp.int32, (rank, rank), 1)
+    line = lax.broadcasted_iota(jnp.int32, (rank, rank), 0)
+    value = work[...]
+    pivots = jnp.sum(jnp.where(lane == line, value, 0.0), axis=1, keepdims=True)
+    unit = jnp.where(lane == line, 1.0, jnp.where(lane < line, value, 0.0))
+    return unit * lax.rsqrt(pivots)
+
+
+def factor_kernel(minor, major, a_far, b_far, e_far, basis, merged_far, ortho, new_basis,
+                  a, b, e, merged, merged_top, merged_rest,
+                  part, half, land_core, quarter, land_minor, land_major, total,
+                  right, quarter_right, land_minor_right, land_major_right, total_right,
+                  work, inverse, send, recv, local):
     dp, core = lax.axis_index("dp"), lax.axis_index("shard")
     q, z = lax.rem(dp, minor), lax.div(dp, minor)
+    loads = [
+        pltpu.make_async_copy(far, near, local.at[i])
+        for i, (far, near) in enumerate(((b_far, b), (a_far, a), (e_far, e)))
+    ]
+    for load in loads:
+        load.start()
     greet(minor, major, True)
-    n_half = half.shape[0]
+
+    rows, columns = merged.shape
+    width = half.shape[1]
+    spans = [(0, width), (width, rows - width)]
+    basis_parts = halves(basis[...].T)
+    loads[0].wait()
+    token_parts = halves(fold(dot(basis_parts, b[...], 1, 1)))
+    loads[1].wait()
+    loads[2].wait()
+    for h, (start, size) in enumerate(spans):
+        value = fold(
+            dot(token_parts, a[:, start:start + size], 1, 0)
+            + dot(basis_parts, e[start:start + size, :], 1, 1)
+        )
+        if size < width:
+            part[h] = jnp.zeros_like(half)
+        part[h, :, :size] = value
+
+    def keep(place, value):
+        merged[place, :] = value
+        top = value.astype(jnp.bfloat16)
+        merged_top[place, :] = top
+        merged_rest[place, :] = (value - top.astype(jnp.float32)).astype(jnp.bfloat16)
+
+    def tile(i, carry):
+        place = rows_at(i, 256)
+        keep(place, dot(a[:, place], b[...], 0, 0) + e[place, :].astype(jnp.float32))
+        return carry
+
+    full = rows // 256
+    cuts = [min(cut, full) for cut in (0, 1, 4, 5, 6)] + [full]
+
+    def tiles(stage):
+        if cuts[stage] < cuts[stage + 1]:
+            lax.fori_loop(cuts[stage], cuts[stage + 1], tile, 0)
+
+    slot = 0
+    copies = [push(part.at[1 - core], land_core, send, recv, slot, dp, 1 - core)]
+    slot += 1
+    tiles(0)
+    arrive(copies)
+    half[...] = part[core] + land_core[...]
+    copies = scatter_minor(minor, half, land_minor, send, recv, slot)
+    slot += minor - 1
+    tiles(1)
+    arrive(copies)
     n_quarter = quarter.shape[0]
     n_own = n_quarter // major
-    arrive([push(part.at[rows_at(1 - core, n_half)], land_core, send, recv, 0, dp, 1 - core)])
-    half[...] = part[rows_at(core, n_half), :] + land_core[...]
-    arrive(scatter_minor(minor, half, land_minor, send, recv, 1))
     value = half[rows_at(q, n_quarter), :]
     for j in range(minor - 1):
         value = value + land_minor[j]
     quarter[...] = value
-    slot = minor
-    arrive(scatter_major(minor, major, quarter, land_major, send, recv, slot))
+    copies = scatter_major(minor, major, quarter, land_major, send, recv, slot)
     slot += major - 1
+    tiles(2)
+    arrive(copies)
     value = quarter[rows_at(z, n_own), :]
     for j in range(major - 1):
         value = value + land_major[j]
-    own = rows_at((core * minor + q) * major + z, n_own)
-    total[own, :] = value
-    arrive(gather(minor, major, True, total, own, send, recv, slot))
+    mine = total.at[core]
+    own = rows_at(q * major + z, n_own)
+    mine[own, :] = value
+    copies = gather(minor, major, True, mine, own, send, recv, slot)
     slot += major - 1
-    own = rows_at(core * minor + q, n_quarter)
-    arrive(gather(minor, major, False, total, own, send, recv, slot))
+    tiles(3)
+    arrive(copies)
+    copies = gather(minor, major, False, mine, rows_at(q, n_quarter), send, recv, slot)
     slot += minor - 1
-    own = rows_at(core, n_half)
-    arrive([push(total.at[own], total.at[own], send, recv, slot, dp, 1 - core)])
-
-
-def sum_left(part, minor, major):
-    rows, rank = part.shape
-    n_half = rows // 2
-    n_quarter = n_half // minor
-    n_own = n_quarter // major
-    copies = 2 + 2 * (minor - 1) + 2 * (major - 1)
-    vmem = pl.BlockSpec(memory_space=pltpu.VMEM)
-    f32 = jnp.float32
-    return pl.pallas_call(
-        functools.partial(left_kernel, minor, major),
-        out_shape=jax.ShapeDtypeStruct((rows, rank), f32),
-        in_specs=[vmem],
-        out_specs=vmem,
-        scratch_shapes=[
-            pltpu.VMEM((n_half, rank), f32),
-            pltpu.VMEM((n_quarter, rank), f32),
-            pltpu.VMEM((n_half, rank), f32),
-            pltpu.VMEM((minor - 1, n_quarter, rank), f32),
-            pltpu.VMEM((major - 1, n_own, rank), f32),
-            pltpu.SemaphoreType.DMA((copies,)),
-            pltpu.SemaphoreType.DMA((copies,)),
-        ],
-        compiler_params=pltpu.CompilerParams(
-            collective_id=0, has_side_effects=True, vmem_limit_bytes=32 * 1024 * 1024
-        ),
-    )(part)
-
-
-def invert_factor(gram, work):
-    rank = gram.shape[0]
-    lane = lax.broadcasted_iota(jnp.int32, (rank, rank), 1)
-    line = lax.broadcasted_iota(jnp.int32, (rank, rank), 0)
-    eye = lane == line
-    trace = jnp.sum(jnp.where(eye, gram, 0.0), keepdims=True)
-    work[:, :rank] = gram + jnp.where(eye, ridge_scale * trace / rank, 0.0)
-    work[:, rank:] = jnp.where(eye, 1.0, 0.0)
-
-    def step(j, carry):
-        row = work[pl.ds(j, 1), :]
-        left = work[:, :rank]
-        column = jnp.sum(jnp.where(lane == j, left, 0.0), axis=1, keepdims=True)
-        pivot = jnp.sum(
-            jnp.where(lane[:1] == j, row[:, :rank], 0.0), axis=1, keepdims=True
-        )
-        scale = jnp.where(line[:, :1] > j, column / pivot, 0.0)
-        work[...] = work[...] - scale * row
-        return carry
-
-    lax.fori_loop(0, rank, step, 0)
-    pivots = jnp.sum(jnp.where(eye, work[:, :rank], 0.0), axis=1, keepdims=True)
-    return work[:, rank:] * lax.rsqrt(pivots)
-
-
-def right_kernel(minor, major, rows, part, left, basis, ortho, quarter, land_minor, land_major,
-                 total, work, inverse, send, recv):
-    dp = lax.axis_index("dp")
-    q, z = lax.rem(dp, minor), lax.div(dp, minor)
-    greet(minor, major, False)
-    n_quarter = quarter.shape[0]
-    n_own = n_quarter // major
-    copies = scatter_minor(minor, part, land_minor, send, recv, 0)
-    summed = left[...]
-    gram = lax.dot_general(
-        summed, summed, (((0,), (0,)), ((), ())), precision=highest,
-        preferred_element_type=jnp.float32,
-    )
-    inverse[...] = invert_factor(gram, work)
-    ortho[...] = lax.dot_general(
-        left[:rows, :], inverse[...], (((1,), (1,)), ((), ())), precision=highest,
-        preferred_element_type=jnp.float32,
-    )
-    arrive(copies)
-    value = part[rows_at(q, n_quarter), :]
+    tiles(4)
+    if full * 256 < rows:
+        place = slice(full * 256, rows)
+        keep(place, dot(a[:, place], b[...], 0, 0) + e[place, :].astype(jnp.float32))
+    store = pltpu.make_async_copy(merged, merged_far, local.at[3])
+    store.start()
+    arrive(copies)
+    copy = push(mine, mine, send, recv, slot, dp, 1 - core)
+    slot += 1
+    copy.wait()
+
+    rank = work.shape[0]
+    for h, (start, size) in enumerate(spans):
+        place = slice(start, start + size)
+        parts = halves(total[h, :, :size])
+        value = fold(dot(parts, merged_top[place, :], 1, 0)) + dot(
+            parts[:rank], merged_rest[place, :], 1, 0
+        )
+        right[...] = value if h == 0 else right[...] + value
+    copies = scatter_minor(minor, right, land_minor_right, send, recv, slot)
+    slot += minor - 1
+    begin_factor(
+        dot(total[0], total[0], 1, 1, highest) + dot(total[1], total[1], 1, 1, highest), work
+    )
+    pairs = rank // 2
+    marks = [0, pairs * 5 // 16, pairs // 2, pairs * 11 // 16, pairs]
+    eliminate(work, marks[0], marks[1])
+    arrive(copies)
+    value = right[rows_at(q, n_quarter), :]
     for j in range(minor - 1):
-        value = value + land_minor[j]
-    quarter[...] = value
-    slot = minor - 1
-    arrive(scatter_major(minor, major, quarter, land_major, send, recv, slot))
+        value = value + land_minor_right[j]
+    quarter_right[...] = value
+    copies = scatter_major(minor, major, quarter_right, land_major_right, send, recv, slot)
     slot += major - 1
-    value = quarter[rows_at(z, n_own), :]
+    eliminate(work, marks[1], marks[2])
+    arrive(copies)
+    value = quarter_right[rows_at(z, n_own), :]
     for j in range(major - 1):
-        value = value + land_major[j]
+        value = value + land_major_right[j]
     own = rows_at(q * major + z, n_own)
-    total[own, :] = value
-    arrive(gather(minor, major, True, total, own, send, recv, slot))
+    total_right[own, :] = value
+    copies = gather(minor, major, True, total_right, own, send, recv, slot)
     slot += major - 1
-    own = rows_at(q, n_quarter)
-    arrive(gather(minor, major, False, total, own, send, recv, slot))
-    basis[...] = lax.dot_general(
-        inverse[...], total[...], (((1,), (0,)), ((), ())), precision=highest,
-        preferred_element_type=jnp.float32,
-    ) * (1.0 / (minor * major))
-
-
-def sum_right(part, left, rows, minor, major):
-    rank, columns = part.shape
+    eliminate(work, marks[2], marks[3])
+    arrive(copies)
+    copies = gather(minor, major, False, total_right, rows_at(q, n_quarter), send, recv, slot)
+    eliminate(work, marks[3], marks[4])
+    inverse[...] = finish_factor(work)
+    for h, (start, size) in enumerate(spans):
+        ortho[start:start + size, :] = dot(
+            total[h, :, :size], inverse[...], 0, 1, highest
+        )
+    arrive(copies)
+    new_basis[...] = dot(inverse[...], total_right[...], 1, 0, highest) * (
+        1.0 / (minor * major)
+    )
+    store.wait()
+
+
+def factors(minor, major, activations, out_grads, error_state, basis):
+    tokens, rows = activations.shape
+    columns, rank = basis.shape
+    width = -(-rows // 256) * 128
     n_quarter = rank // minor
     n_own = n_quarter // major
-    copies = 2 * (minor - 1) + 2 * (major - 1)
-    vmem = pl.BlockSpec(memory_space=pltpu.VMEM)
-    f32 = jnp.float32
+    copies = 2 + 4 * (minor - 1) + 4 * (major - 1)
+    near = pl.BlockSpec(memory_space=pltpu.VMEM)
+    far = pl.BlockSpec(memory_space=pl.ANY)
+    f32, bf16 = jnp.float32, jnp.bfloat16
     return pl.pallas_call(
-        functools.partial(right_kernel, minor, major, rows),
+        functools.partial(factor_kernel, minor, major),
         out_shape=(
+            jax.ShapeDtypeStruct((rows, columns), f32),
+            jax.ShapeDtypeStruct((rows, rank), f32),
             jax.ShapeDtypeStruct((rank, columns), f32),
-            jax.ShapeDtypeStruct((rows, rank), f32),
         ),
-        in_specs=[vmem, vmem],
-        out_specs=(vmem, vmem),
+        in_specs=[far, far, far, near],
+        out_specs=(far, near, near),
         scratch_shapes=[
+            pltpu.VMEM((tokens, rows), bf16),
+            pltpu.VMEM((tokens, columns), bf16),
+            pltpu.VMEM((rows, columns), bf16),
+            pltpu.VMEM((rows, columns), f32),
+            pltpu.VMEM((rows, columns), bf16),
+            pltpu.VMEM((rows, columns), bf16),
+            pltpu.VMEM((2, rank, width), f32),
+            pltpu.VMEM((rank, width), f32),
+            pltpu.VMEM((rank, width), f32),
+            pltpu.VMEM((n_quarter, width), f32),
+            pltpu.VMEM((minor - 1, n_quarter, width), f32),
+            pltpu.VMEM((major - 1, n_own, width), f32),
+            pltpu.VMEM((2, rank, width), f32),
+            pltpu.VMEM((rank, columns), f32),
             pltpu.VMEM((n_quarter, columns), f32),
             pltpu.VMEM((minor - 1, n_quarter, columns), f32),
             pltpu.VMEM((major - 1, n_own, columns), f32),
             pltpu.VMEM((rank, columns), f32),
-            pltpu.VMEM((rank, 2 * rank), f32),
+            pltpu.VMEM((rank, rank), f32),
             pltpu.VMEM((rank, rank), f32),
             pltpu.SemaphoreType.DMA((copies,)),
             pltpu.SemaphoreType.DMA((copies,)),
+            pltpu.SemaphoreType.DMA((4,)),
         ],
         compiler_params=pltpu.CompilerParams(
-            collective_id=1, has_side_effects=True, vmem_limit_bytes=48 * 1024 * 1024
+            collective_id=0, has_side_effects=True, vmem_limit_bytes=58 * 1024 * 1024
         ),
-    )(part, left)
+    )(activations, out_grads, error_state, basis)
 
 
 def pushed(minor, major, activations, out_grads, error_state, basis, master, first_moment,
            second_moment):
-    product = lax.dot_general(
-        activations, out_grads, (((0,), (0,)), ((), ())), preferred_element_type=jnp.float32
-    )
-    merged = product + error_state.astype(jnp.float32)
-    rows = merged.shape[0]
-    chunk = 16 * minor * major
-    padded = -(-rows // chunk) * chunk
-    part = jnp.dot(merged, basis, precision=high)
-    left = sum_left(jnp.pad(part, ((0, padded - rows), (0, 0))), minor, major)
-    right = lax.dot_general(left[:rows], merged, (((0,), (0,)), ((), ())), precision=high)
-    basis_rows, orthonormal = sum_right(right, left, rows, minor, major)
+    merged, orthonormal, basis_rows = factors(
+        minor, major, activations, out_grads, error_state, basis
+    )
     decompressed = jnp.dot(orthonormal, basis_rows, precision=high)
     new_error = (merged - decompressed).astype(jnp.bfloat16)
     rows_dev = master.shape[0]

time: 97.1 us -> 89.9 us (0.926)
  matrix products: 23.8 us -> 12.2 us
  local copies, waits for them, and re-layouts: 4.36 us -> 12.2 us
  Pallas kernels: 65.9 us -> 62.3 us
    dot_general x3 -> x0, matrix products: 15.7 us -> none  [the longest x1 10 us: pushed(): lax.dot_general(activations, out_grads, (((0,), (0,)), ((), ())), preferr...]
    unnamed x10 -> x12, local copies, waits for them, and re-layouts: 4.29 us -> 12.2 us
    dot_general x1, matrix products: 4.89 us -> 9.32 us  [pushed(): decompressed = jnp.dot(orthonormal, basis_rows, precision=high)]
    pallas_call x2 -> x1, Pallas kernels: 65.9 us -> 62.3 us  [factors(): pl.pallas_call(functools.partial(factor_kernel, minor, major), out_shape=...]
where the time goes in v2:
time: 89.9 us; the launch traced here: 89.5 us
  Pallas kernels  62.3 us (69%)
  local copies, waits for them, and re-layouts  12.2 us (14%)
  matrix products  12.2 us (14%)
  blocking collectives  2.16 us (2%)
    pallas_call x1, Pallas kernels, factors(): pl.pallas_call(functools.partial(factor_kernel, minor, major), out_shape=...  62.3 us
    unnamed x12, local copies, waits for them, and re-layouts  12.2 us
    dot_general x1, matrix products, pushed(): decompressed = jnp.dot(orthonormal, basis_rows, precision=high)  9.32 us
    dot_general x1, matrix products, pushed(): jnp.dot(lax.dynamic_slice_in_dim(orthonormal, row_offset, rows_dev, 0), b...  2.91 us
    all_gather x1, blocking collectives, pushed(): lax.all_gather(new_master.astype(jnp.bfloat16), 'shard', axis=1, tiled=True)  2.16 us

profile of v2, /device:TPU:0, one launch (start us, length us, event | category | flops | bytes accessed | tf_op | source)
XLA Modules:
  0.0 89.5 jit_solution(2552039641667768656)
XLA Ops:
  0.6 3.9 %copy.15.b_far = bf16[1024,992]{1,0:T(8,128)(2,1)} copy(bf16[1024,992]{0,1:T(8,128)(2,1)} %param.8) | data formatting | bytes 4063232 | tf_op args[1]
  4.6 6.5 %copy.14.a_far = bf16[1024,1984]{1,0:T(8,128)(2,1)} copy(bf16[1024,1984]{0,1:T(8,128)(2,1)} %param.7) | data formatting | bytes 8126464 | tf_op args[0]
  11.0 62.3 %shard_map.126 = (f32[1984,992]{1,0:T(8,128)}, f32[1984,128]{1,0:T(8,128)}, f32[128,992]{1,0:T(8,128)}) custom-call(bf16[1024,1984]{1,0:T(8,128)(2,1)} %copy.14.a_far, bf16[1024,992]{1,0:T(8,128)(2,1)} %copy.15.b_far, bf16[1984,992]{1,0:T(8,128)(2,1)} %e_far.1, f32[992,128]{1,0:T(8,128)} %basis.1), custom_call_target="tpu_custom_call" | custom-call | tf_op jit(solution)/shard_map/pallas_call | solution.py:345
  73.3 0.0 copy-start
  73.3 0.0 copy-start.1
  73.3 0.0 copy-start.2
  73.4 0.0 copy-start.3
  73.4 9.3 %subtract_convert_fusion = bf16[1984,992]{1,0:T(8,128)(2,1)} fusion(f32[1984,992]{1,0:T(8,128)} %get-tuple-element.12, f32[1984,128]{1,0:T(8,128)} %get-tuple-element.10, f32[128,992]{1,0:T(8,128)} %get-tuple-element.11), kind=kOutput, calls=%fused_computation | convolution fusion | flops 1515458560 | bytes 13332480 | tf_op jit(solution)/shard_map/dot_general | solution.py:390
  82.7 0.0 copy-done
  82.7 1.0 %copy.16 = f32[992,128]{1,0:T(8,128)} copy(f32[992,128]{0,1:T(8,128)S(1)} %bitcast.4) | data formatting | bytes 1015808
  83.7 0.0 copy-done.1
  83.7 0.0 copy-done.2
  83.7 0.0 copy-done.3
  83.7 2.9 %fusion.4 = (bf16[124,992]{0,1:T(8,128)(2,1)S(1)}, f32[124,992]{0,1:T(8,128)}, f32[124,992]{0,1:T(8,128)}, f32[124,992]{0,1:T(8,128)}, f32[124,992]{0,1:T(8,128)}) fusion(f32[124,992]{0,1:T(8,128)S(1)} %copy-done.1, f32[124,992]{0,1:T(8,128)S(1)} %copy-done.2, f32[124,992]{0,1:T(8,128)S(1)} %copy-done.3, f32[128,992]{1,0:T(8,128)S(1)} %copy-done, ...), kind=kOutput, calls=%fused_computation.8 | convolution fusion | flops 95946240 | bytes 4263684 | tf_op jit(solution)/shard_map/dot_general | solution.py:394
  86.6 2.2 %all_gather.3 = bf16[124,1984]{0,1:T(8,128)(2,1)S(1)} all-gather(bf16[124,992]{0,1:T(8,128)(2,1)S(1)} %get-tuple-element.20), channel_id=1, replica_groups=mesh['dp'=16,'shard'=2] {'shard'}, dimensions={1}, use_global_device_ids=true | all-gather | bytes 738048 | tf_op jit(solution)/shard_map/all_gather | solution.py:398
  88.8 0.8 copy.18
Async XLA Ops:
  73.3 9.4 %copy-start = (f32[128,992]{1,0:T(8,128)S(1)}, f32[128,992]{1,0:T(8,128)}, u32[]{:S(2)}) copy-start(f32[128,992]{1,0:T(8,128)} %get-tuple-element.11) | copy-start | bytes 1523716
  73.3 10.4 %copy-start.1 = (f32[124,992]{0,1:T(8,128)S(1)}, f32[124,992]{0,1:T(8,128)}, u32[]{:S(2)}) copy-start(f32[124,992]{0,1:T(8,128)} %param.11) | copy-start | bytes 1476100
  73.3 10.3 %copy-start.2 = (f32[124,992]{0,1:T(8,128)S(1)}, f32[124,992]{0,1:T(8,128)}, u32[]{:S(2)}) copy-start(f32[124,992]{0,1:T(8,128)} %param.12) | copy-start | bytes 1476100
  73.4 10.3 %copy-start.3 = (f32[124,992]{0,1:T(8,128)S(1)}, f32[124,992]{0,1:T(8,128)}, u32[]{:S(2)}) copy-start(f32[124,992]{0,1:T(8,128)} %param.13) | copy-start | bytes 1476100

commit v3 on v2

--- a/solution.py
+++ b/solution.py
@@ -191,7 +191,7 @@
     return unit * lax.rsqrt(pivots)
 
 
-def factor_kernel(minor, major, a_far, b_far, e_far, basis, merged_far, ortho, new_basis,
+def factor_kernel(minor, major, a_far, b_far, e_far, basis, error_far, ortho, new_basis,
                   a, b, e, merged, merged_top, merged_rest,
                   part, half, land_core, quarter, land_minor, land_major, total,
                   right, quarter_right, land_minor_right, land_major_right, total_right,
@@ -207,21 +207,27 @@
     greet(minor, major, True)
 
     rows, columns = merged.shape
-    width = half.shape[1]
+    count = half.shape[0]
+    piece = half.shape[2]
+    width = count * piece
     spans = [(0, width), (width, rows - width)]
+    merged_top[rows:, :] = jnp.zeros_like(merged_top[rows:, :])
+    merged_rest[rows:, :] = jnp.zeros_like(merged_rest[rows:, :])
     basis_parts = halves(basis[...].T)
     loads[0].wait()
-    token_parts = halves(fold(dot(basis_parts, b[...], 1, 1)))
+    token_parts = halves(fold(dot(basis_parts, b[...], 1, 0)))
     loads[1].wait()
     loads[2].wait()
     for h, (start, size) in enumerate(spans):
         value = fold(
-            dot(token_parts, a[:, start:start + size], 1, 0)
+            dot(token_parts, a[start:start + size, :], 1, 1)
             + dot(basis_parts, e[start:start + size, :], 1, 1)
         )
-        if size < width:
-            part[h] = jnp.zeros_like(half)
-        part[h, :, :size] = value
+        for k in range(count):
+            held = min(piece, size - k * piece)
+            if held < piece:
+                part[h, k] = jnp.zeros(part.shape[2:], jnp.float32)
+            part[h, k, :, :held] = value[:, k * piece:k * piece + held]
 
     def keep(place, value):
         merged[place, :] = value
@@ -231,105 +237,143 @@
 
     def tile(i, carry):
         place = rows_at(i, 256)
-        keep(place, dot(a[:, place], b[...], 0, 0) + e[place, :].astype(jnp.float32))
+        keep(place, dot(a[place, :], b[...], 1, 1) + e[place, :].astype(jnp.float32))
         return carry
 
     full = rows // 256
-    cuts = [min(cut, full) for cut in (0, 1, 4, 5, 6)] + [full]
+    cuts = [min(cut, full) for cut in (0, 2, 3, 4)] + [full]
 
     def tiles(stage):
         if cuts[stage] < cuts[stage + 1]:
             lax.fori_loop(cuts[stage], cuts[stage + 1], tile, 0)
 
-    slot = 0
-    copies = [push(part.at[1 - core], land_core, send, recv, slot, dp, 1 - core)]
-    slot += 1
-    tiles(0)
-    arrive(copies)
-    half[...] = part[core] + land_core[...]
-    copies = scatter_minor(minor, half, land_minor, send, recv, slot)
-    slot += minor - 1
-    tiles(1)
-    arrive(copies)
-    n_quarter = quarter.shape[0]
-    n_own = n_quarter // major
-    value = half[rows_at(q, n_quarter), :]
-    for j in range(minor - 1):
-        value = value + land_minor[j]
-    quarter[...] = value
-    copies = scatter_major(minor, major, quarter, land_major, send, recv, slot)
-    slot += major - 1
-    tiles(2)
-    arrive(copies)
-    value = quarter[rows_at(z, n_own), :]
-    for j in range(major - 1):
-        value = value + land_major[j]
-    mine = total.at[core]
-    own = rows_at(q * major + z, n_own)
-    mine[own, :] = value
-    copies = gather(minor, major, True, mine, own, send, recv, slot)
-    slot += major - 1
-    tiles(3)
-    arrive(copies)
-    copies = gather(minor, major, False, mine, rows_at(q, n_quarter), send, recv, slot)
-    slot += minor - 1
-    tiles(4)
+    slots = iter(range(send.shape[0]))
+
+    def take(number):
+        return [next(slots) for unused in range(number)][0]
+
+    def all_sum(source, begin, land_one, middle, land_two, result, between):
+        n_quarter = middle.shape[1]
+        n_own = n_quarter // major
+        moving = []
+        for k in range(count):
+            begin(k)
+            moving.append(
+                scatter_minor(minor, source.at[k], land_one.at[k], send, recv, take(minor - 1))
+            )
+        between(0)
+        for k in range(count):
+            arrive(moving[k])
+            value = source[k, rows_at(q, n_quarter), :]
+            for j in range(minor - 1):
+                value = value + land_one[k, j]
+            middle[k] = value
+            moving[k] = scatter_major(
+                minor, major, middle.at[k], land_two.at[k], send, recv, take(major - 1)
+            )
+        between(1)
+        own = rows_at(q * major + z, n_own)
+        for k in range(count):
+            arrive(moving[k])
+            value = middle[k, rows_at(z, n_own), :]
+            for j in range(major - 1):
+                value = value + land_two[k, j]
+            result(k)[own, :] = value
+            moving[k] = gather(minor, major, True, result(k), own, send, recv, take(major - 1))
+        between(2)
+        own = rows_at(q, n_quarter)
+        for k in range(count):
+            arrive(moving[k])
+            moving[k] = gather(minor, major, False, result(k), own, send, recv, take(minor - 1))
+        between(3)
+        return moving
+
+    crossing = [
+        push(part.at[1 - core, k], land_core.at[k], send, recv, take(1), dp, 1 - core)
+        for k in range(count)
+    ]
+
+    def begin_left(k):
+        arrive([crossing[k]])
+        half[k] = part[core, k] + land_core[k]
+
+    moving = all_sum(
+        half, begin_left, land_minor, quarter, land_major, lambda k: total.at[core, k], tiles
+    )
+    crossing = []
+    for k in range(count):
+        arrive(moving[k])
+        mine = total.at[core, k]
+        crossing.append(push(mine, mine, send, recv, take(1), dp, 1 - core))
     if full * 256 < rows:
         place = slice(full * 256, rows)
-        keep(place, dot(a[:, place], b[...], 0, 0) + e[place, :].astype(jnp.float32))
-    store = pltpu.make_async_copy(merged, merged_far, local.at[3])
-    store.start()
-    arrive(copies)
-    copy = push(mine, mine, send, recv, slot, dp, 1 - core)
-    slot += 1
-    copy.wait()
+        keep(place, dot(a[place, :], b[...], 1, 1) + e[place, :].astype(jnp.float32))
 
     rank = work.shape[0]
-    for h, (start, size) in enumerate(spans):
-        place = slice(start, start + size)
-        parts = halves(total[h, :, :size])
-        value = fold(dot(parts, merged_top[place, :], 1, 0)) + dot(
-            parts[:rank], merged_rest[place, :], 1, 0
-        )
-        right[...] = value if h == 0 else right[...] + value
-    copies = scatter_minor(minor, right, land_minor_right, send, recv, slot)
-    slot += minor - 1
-    begin_factor(
-        dot(total[0], total[0], 1, 1, highest) + dot(total[1], total[1], 1, 1, highest), work
-    )
+    across = right.shape[2]
+    bands = [(k * across, min(across, columns - k * across)) for k in range(count)]
+
+    def joined(h):
+        return jnp.concatenate([total[h, k] for k in range(count)], axis=1)
+
+    def product(parts, place, start, size):
+        return fold(dot(parts, merged_top[place, start:start + size], 1, 0)) + dot(
+            parts[:rank], merged_rest[place, start:start + size], 1, 0
+        )
+
+    parts = halves(joined(core))
+    for k, (start, size) in enumerate(bands):
+        if size < across:
+            right[k] = jnp.zeros(right.shape[1:], jnp.float32)
+        right[k, :, :size] = product(parts, rows_at(core, width), start, size)
+    arrive(crossing)
+    parts = halves(joined(1 - core))
+
+    def begin_right(k):
+        start, size = bands[k]
+        right[k, :, :size] += product(parts, rows_at(1 - core, width), start, size)
+
     pairs = rank // 2
-    marks = [0, pairs * 5 // 16, pairs // 2, pairs * 11 // 16, pairs]
-    eliminate(work, marks[0], marks[1])
-    arrive(copies)
-    value = right[rows_at(q, n_quarter), :]
-    for j in range(minor - 1):
-        value = value + land_minor_right[j]
-    quarter_right[...] = value
-    copies = scatter_major(minor, major, quarter_right, land_major_right, send, recv, slot)
-    slot += major - 1
-    eliminate(work, marks[1], marks[2])
-    arrive(copies)
-    value = quarter_right[rows_at(z, n_own), :]
-    for j in range(major - 1):
-        value = value + land_major_right[j]
-    own = rows_at(q * major + z, n_own)
-    total_right[own, :] = value
-    copies = gather(minor, major, True, total_right, own, send, recv, slot)
-    slot += major - 1
-    eliminate(work, marks[2], marks[3])
-    arrive(copies)
-    copies = gather(minor, major, False, total_right, rows_at(q, n_quarter), send, recv, slot)
-    eliminate(work, marks[3], marks[4])
+    marks = [0, pairs * 3 // 16, pairs * 5 // 16, pairs * 7 // 16, pairs]
+
+    def factor(stage):
+        if stage == 0:
+            first, second = joined(0), joined(1)
+            begin_factor(
+                dot(first, first, 1, 1, highest) + dot(second, second, 1, 1, highest), work
+            )
+        eliminate(work, marks[stage], marks[stage + 1])
+
+    moving = all_sum(
+        right, begin_right, land_minor_right, quarter_right, land_major_right,
+        lambda k: total_right.at[k], factor,
+    )
     inverse[...] = finish_factor(work)
     for h, (start, size) in enumerate(spans):
-        ortho[start:start + size, :] = dot(
-            total[h, :, :size], inverse[...], 0, 1, highest
-        )
-    arrive(copies)
-    new_basis[...] = dot(inverse[...], total_right[...], 1, 0, highest) * (
-        1.0 / (minor * major)
-    )
-    store.wait()
+        ortho[start:start + size, :] = dot(joined(h), inverse[...], 0, 1, highest)[:size]
+    for k, (start, size) in enumerate(bands):
+        arrive(moving[k])
+        new_basis[:, start:start + size] = dot(
+            inverse[...], total_right[k], 1, 0, highest
+        )[:, :size] * (1.0 / (minor * major))
+    value = new_basis[...]
+    top = value.astype(jnp.bfloat16)
+    rest = (value - top.astype(jnp.float32)).astype(jnp.bfloat16)
+    basis_stack = jnp.concatenate([top, rest, top], axis=0)
+    stores = []
+    step_rows = -(-rows // 64) * 16
+    for i, start in enumerate(range(0, rows, step_rows)):
+        place = slice(start, min(start + step_rows, rows))
+        value = ortho[place, :]
+        top = value.astype(jnp.bfloat16)
+        rest = (value - top.astype(jnp.float32)).astype(jnp.bfloat16)
+        stack = jnp.concatenate([top, top, rest], axis=1)
+        e[place, :] = (merged[place, :] - dot(stack, basis_stack, 1, 0)).astype(jnp.bfloat16)
+        store = pltpu.make_async_copy(e.at[place], error_far.at[place], local.at[3 + i])
+        store.start()
+        stores.append(store)
+    for store in stores:
+        store.wait()
 
 
 def factors(minor, major, activations, out_grads, error_state, basis):
@@ -338,57 +382,58 @@
     width = -(-rows // 256) * 128
     n_quarter = rank // minor
     n_own = n_quarter // major
-    copies = 2 + 4 * (minor - 1) + 4 * (major - 1)
+    count = 2 if width % 256 == 0 else 1
+    piece = width // count
+    across = -(-columns // (128 * count)) * 128
+    copies = count * (2 + 4 * (minor - 1) + 4 * (major - 1))
     near = pl.BlockSpec(memory_space=pltpu.VMEM)
     far = pl.BlockSpec(memory_space=pl.ANY)
     f32, bf16 = jnp.float32, jnp.bfloat16
     return pl.pallas_call(
         functools.partial(factor_kernel, minor, major),
         out_shape=(
-            jax.ShapeDtypeStruct((rows, columns), f32),
+            jax.ShapeDtypeStruct((rows, columns), bf16),
             jax.ShapeDtypeStruct((rows, rank), f32),
             jax.ShapeDtypeStruct((rank, columns), f32),
         ),
         in_specs=[far, far, far, near],
         out_specs=(far, near, near),
         scratch_shapes=[
-            pltpu.VMEM((tokens, rows), bf16),
-            pltpu.VMEM((tokens, columns), bf16),
+            pltpu.VMEM((rows, tokens), bf16),
+            pltpu.VMEM((columns, tokens), bf16),
             pltpu.VMEM((rows, columns), bf16),
             pltpu.VMEM((rows, columns), f32),
-            pltpu.VMEM((rows, columns), bf16),
-            pltpu.VMEM((rows, columns), bf16),
-            pltpu.VMEM((2, rank, width), f32),
-            pltpu.VMEM((rank, width), f32),
-            pltpu.VMEM((rank, width), f32),
-            pltpu.VMEM((n_quarter, width), f32),
-            pltpu.VMEM((minor - 1, n_quarter, width), f32),
-            pltpu.VMEM((major - 1, n_own, width), f32),
-            pltpu.VMEM((2, rank, width), f32),
-            pltpu.VMEM((rank, columns), f32),
-            pltpu.VMEM((n_quarter, columns), f32),
-            pltpu.VMEM((minor - 1, n_quarter, columns), f32),
-            pltpu.VMEM((major - 1, n_own, columns), f32),
-            pltpu.VMEM((rank, columns), f32),
+            pltpu.VMEM((2 * width, columns), bf16),
+            pltpu.VMEM((2 * width, columns), bf16),
+            pltpu.VMEM((2, count, rank, piece), f32),
+            pltpu.VMEM((count, rank, piece), f32),
+            pltpu.VMEM((count, rank, piece), f32),
+            pltpu.VMEM((count, n_quarter, piece), f32),
+            pltpu.VMEM((count, minor - 1, n_quarter, piece), f32),
+            pltpu.VMEM((count, major - 1, n_own, piece), f32),
+            pltpu.VMEM((2, count, rank, piece), f32),
+            pltpu.VMEM((count, rank, across), f32),
+            pltpu.VMEM((count, n_quarter, across), f32),
+            pltpu.VMEM((count, minor - 1, n_quarter, across), f32),
+            pltpu.VMEM((count, major - 1, n_own, across), f32),
+            pltpu.VMEM((count, rank, across), f32),
             pltpu.VMEM((rank, rank), f32),
             pltpu.VMEM((rank, rank), f32),
             pltpu.SemaphoreType.DMA((copies,)),
             pltpu.SemaphoreType.DMA((copies,)),
-            pltpu.SemaphoreType.DMA((4,)),
+            pltpu.SemaphoreType.DMA((7,)),
         ],
         compiler_params=pltpu.CompilerParams(
             collective_id=0, has_side_effects=True, vmem_limit_bytes=58 * 1024 * 1024
         ),
-    )(activations, out_grads, error_state, basis)
+    )(activations.T, out_grads.T, error_state, basis)
 
 
 def pushed(minor, major, activations, out_grads, error_state, basis, master, first_moment,
            second_moment):
-    merged, orthonormal, basis_rows = factors(
+    new_error, orthonormal, basis_rows = factors(
         minor, major, activations, out_grads, error_state, basis
     )
-    decompressed = jnp.dot(orthonormal, basis_rows, precision=high)
-    new_error = (merged - decompressed).astype(jnp.bfloat16)
     rows_dev = master.shape[0]
     row_offset = lax.axis_index("dp") * rows_dev
     update = jnp.dot(

time: 89.9 us -> 73 us (0.81)
  matrix products: 12.2 us -> 3.25 us
  local copies, waits for them, and re-layouts: 12.2 us -> 4.79 us
    dot_general x1 -> x0, matrix products: 9.32 us -> none  [pushed(): decompressed = jnp.dot(orthonormal, basis_rows, precision=high)]
    unnamed x12 -> x11, local copies, waits for them, and re-layouts: 12.2 us -> 4.79 us
where the time goes in v3:
time: 73 us; the launch traced here: 72.8 us
  Pallas kernels  62 us (85%)
  local copies, waits for them, and re-layouts  4.79 us (7%)
  matrix products  3.25 us (4%)
  blocking collectives  2.16 us (3%)
    pallas_call x1, Pallas kernels, factors(): pl.pallas_call(functools.partial(factor_kernel, minor, major), out_shape=...  62 us
    unnamed x11, local copies, waits for them, and re-layouts  4.79 us
    dot_general x1, matrix products, pushed(): jnp.dot(lax.dynamic_slice_in_dim(orthonormal, row_offset, rows_dev, 0), b...  3.25 us
    all_gather x1, blocking collectives, pushed(): lax.all_gather(new_master.astype(jnp.bfloat16), 'shard', axis=1, tiled=True)  2.16 us

profile of v3, /device:TPU:0, one launch (start us, length us, event | category | flops | bytes accessed | tf_op | source)
XLA Modules:
  0.0 72.8 jit_solution(14088637029207676637)
XLA Ops:
  0.6 0.0 copy-start.1
  0.7 0.0 copy-start.2
  0.7 0.0 copy-start.3
  0.7 62.0 %shard_map.126 = (bf16[1984,992]{1,0:T(8,128)(2,1)}, f32[1984,128]{1,0:T(8,128)}, f32[128,992]{1,0:T(8,128)}) custom-call(bf16[1984,1024]{1,0:T(8,128)(2,1)} %bitcast.4, bf16[992,1024]{1,0:T(8,128)(2,1)} %bitcast.6, bf16[1984,992]{1,0:T(8,128)(2,1)} %e_far.1, f32[992,128]{1,0:T(8,128)} %basis.1), custom_call_target="tpu_custom_call" | custom-call | tf_op jit(solution)/shard_map/pallas_call | solution.py:392
  62.6 2.0 %copy.14 = f32[992,128]{1,0:T(8,128)} copy(f32[992,128]{0,1:T(8,128)} %bitcast.5) | data formatting | bytes 1015808
  64.7 0.0 copy-done.1
  64.7 0.0 copy-done.2
  64.7 0.0 copy-done.3
  64.7 0.0 copy-start
  64.7 3.3 %fusion.4 = (bf16[124,992]{0,1:T(8,128)(2,1)S(1)}, f32[124,992]{0,1:T(8,128)}, f32[124,992]{0,1:T(8,128)}, f32[124,992]{0,1:T(8,128)}, f32[124,992]{0,1:T(8,128)}) fusion(f32[124,992]{0,1:T(8,128)S(1)} %copy-done.1, f32[124,992]{0,1:T(8,128)S(1)} %copy-done.2, f32[124,992]{0,1:T(8,128)S(1)} %copy-done.3, f32[128,992]{1,0:T(8,128)} %get-tuple-element.11, ...), kind=kOutput, calls=%fused_computation.7 | convolution fusion | flops 95946240 | bytes 4280068 | tf_op jit(solution)/shard_map/dot_general | solution.py:439
  67.9 2.2 %all_gather.3 = bf16[124,1984]{0,1:T(8,128)(2,1)S(1)} all-gather(bf16[124,992]{0,1:T(8,128)(2,1)S(1)} %get-tuple-element.20), channel_id=1, replica_groups=mesh['dp'=16,'shard'=2] {'shard'}, dimensions={1}, use_global_device_ids=true | all-gather | bytes 738048 | tf_op jit(solution)/shard_map/all_gather | solution.py:443
  70.1 0.8 %copy.17 = bf16[124,1984]{0,1:T(8,128)(2,1)} copy(bf16[124,1984]{0,1:T(8,128)(2,1)S(1)} %all_gather.3) | data formatting | bytes 984064
  70.9 0.0 copy-done
  70.9 2.0 %copy.18 = bf16[1984,992]{1,0:T(8,128)(2,1)} copy(bf16[1984,992]{1,0:T(8,128)(2,1)S(1)} %copy-done) | data formatting | bytes 7872512
Async XLA Ops:
  0.6 64.0 %copy-start.1 = (f32[124,992]{0,1:T(8,128)S(1)}, f32[124,992]{0,1:T(8,128)}, u32[]{:S(2)}) copy-start(f32[124,992]{0,1:T(8,128)} %param.11) | copy-start | bytes 1476100
  0.7 64.0 %copy-start.2 = (f32[124,992]{0,1:T(8,128)S(1)}, f32[124,992]{0,1:T(8,128)}, u32[]{:S(2)}) copy-start(f32[124,992]{0,1:T(8,128)} %param.12) | copy-start | bytes 1476100
  0.7 64.0 %copy-start.3 = (f32[124,992]{0,1:T(8,128)S(1)}, f32[124,992]{0,1:T(8,128)}, u32[]{:S(2)}) copy-start(f32[124,992]{0,1:T(8,128)} %param.13) | copy-start | bytes 1476100
  64.7 6.2 %copy-start = (bf16[1984,992]{1,0:T(8,128)(2,1)S(1)}, bf16[1984,992]{1,0:T(8,128)(2,1)}, u32[]{:S(2)}) copy-start(bf16[1984,992]{1,0:T(8,128)(2,1)} %get-tuple-element.33) | copy-start | bytes 11808772
